TPU v7x, 512 devices: a whole 4x8x8 slice. The times are simulated.
512 devices in a mesh: gx: 8 (over y), gy: 8 (over z_hi, core), gz: 8 (over x, z_lo).
Axes of the slice: x: 4, y: 8, z: 8 (z_hi: 4, z_lo: 2; z = z_hi * 2 + z_lo), core: 2. Of those that a mesh axis runs over, the one named last changes fastest.
Arguments:
- features: bfloat16 [8, 8, 8, 32, 49, 128], P('gx', 'gy', 'gz'), may hold values from -6 to 6
- border_atoms: int32 [8, 8, 8, 4], P('gx', 'gy', 'gz'), may hold values from 0 to 31, as said below
- inner_source: int32 [8, 8, 8, 128], P('gx', 'gy', 'gz'), may hold values from 0 to 31
- inner_target: int32 [8, 8, 8, 128], P('gx', 'gy', 'gz'), may hold values from 0 to 31
- inner_rotation: int32 [8, 8, 8, 128], P('gx', 'gy', 'gz'), may hold values from 0 to 255
- inner_count: int32 [8, 8, 8], P('gx', 'gy', 'gz'), may hold values from 64 to 128, as said below
- cross_source: int32 [8, 8, 8, 128], P('gx', 'gy', 'gz'), may hold values from 0 to 107, as said below
- cross_target: int32 [8, 8, 8, 128], P('gx', 'gy', 'gz'), may hold values from 0 to 31
- cross_rotation: int32 [8, 8, 8, 2, 128], P('gx', 'gy', 'gz'), may hold values from 0 to 255
- cross_count: int32 [8, 8, 8], P('gx', 'gy', 'gz'), may hold values from 64 to 128, as said below
- rotations: bfloat16 [49, 49, 256], replicated, as said below
- order_zero: bfloat16 [896, 896], P(('gy', 'gz')), may hold values from -0.1875 to 0.1875
- order_one: bfloat16 [2, 768, 768], P(None, ('gy', 'gz')), may hold values from -0.15625 to 0.15625
- order_two: bfloat16 [2, 640, 640], P(None, ('gy', 'gz')), may hold values from -0.15625 to 0.15625
Outputs:
- updated: bfloat16 [8, 8, 8, 32, 49, 128], P('gx', 'gy', 'gz')
Inputs may be any that keep to these rules, and one draw needn't show every extreme that they name: `border_atoms`: 4 different atoms of the cell. `inner_count`: edges at positions below the count are live; some cell has all 128 live. `cross_count`: edges at positions below the count are live; some cell has all 128 live. `cross_source`: a row s * 4 + t of around with s never 13, the cell itself. An entry rotations[i, j, r] is zero unless i and j have the same degree.
All inputs are finite; a program needn't handle non-finite values.
Results may differ from a plain program's by a relative error of at most 0.006.
Values may be sent and summed in bfloat16 or wider, within the bound.
No kernel may reach another device: no remote copies, remote signals or barrier semaphores. Data moves between devices by JAX's collectives and lax.ppermute only.
A program may use at most 128 MiB of HBM per device.

v0:
```python
import math
import jax
import jax.numpy as jnp
import numpy as np
from jax import lax
from jax.sharding import PartitionSpec as P

LMAX = 6


def extended(block, sides, width):
    for axis, dim in sides:
        count = lax.axis_size(axis)
        forward = [(i, i + 1) for i in range(count - 1)]
        forward.append((count - 1, 0))
        backward = [(target, source) for source, target in forward]
        low = lax.ppermute(
            lax.slice_in_dim(block, block.shape[dim] - width, None, axis=dim), axis, forward
        )
        high = lax.ppermute(lax.slice_in_dim(block, 0, width, axis=dim), axis, backward)
        block = jnp.concatenate([low, block, high], axis=dim)
    return block


def kept_rows(top_degree):
    listing = [d * d + d for d in range(top_degree + 1)]
    for shift in (1, -1, 2, -2):
        listing = listing + [d * d + d + shift for d in range(abs(shift), top_degree + 1)]
    return np.array(listing, dtype=np.int32)


def conv_messages(sources, chosen, full_zero, full_one, full_two):
    row_total = sources.shape[0]
    channels = sources.shape[2]
    size_zero = LMAX + 1
    size_one = LMAX
    size_two = LMAX - 1
    turned = jnp.einsum("nrj,njc->nrc", chosen, sources, preferred_element_type=jnp.float32).astype(
        jnp.bfloat16
    )
    zero_part = turned[:, :size_zero].reshape(row_total, size_zero * channels)
    plus_one = turned[:, size_zero : size_zero + size_one].reshape(row_total, size_one * channels)
    minus_one = turned[:, size_zero + size_one : size_zero + 2 * size_one].reshape(
        row_total, size_one * channels
    )
    two_start = size_zero + 2 * size_one
    plus_two = turned[:, two_start : two_start + size_two].reshape(row_total, size_two * channels)
    minus_two = turned[:, two_start + size_two : two_start + 2 * size_two].reshape(
        row_total, size_two * channels
    )
    out_zero = jnp.dot(zero_part, full_zero, preferred_element_type=jnp.float32)
    out_plus1 = jnp.dot(plus_one, full_one[0], preferred_element_type=jnp.float32) - jnp.dot(
        minus_one, full_one[1], preferred_element_type=jnp.float32
    )
    out_minus1 = jnp.dot(minus_one, full_one[0], preferred_element_type=jnp.float32) + jnp.dot(
        plus_one, full_one[1], preferred_element_type=jnp.float32
    )
    out_plus2 = jnp.dot(plus_two, full_two[0], preferred_element_type=jnp.float32) - jnp.dot(
        minus_two, full_two[1], preferred_element_type=jnp.float32
    )
    out_minus2 = jnp.dot(minus_two, full_two[0], preferred_element_type=jnp.float32) + jnp.dot(
        plus_two, full_two[1], preferred_element_type=jnp.float32
    )
    pieces = [out_zero, out_plus1, out_minus1, out_plus2, out_minus2]
    mixed = jnp.concatenate(
        [piece.reshape(row_total, -1, channels) for piece in pieces], axis=1
    ).astype(jnp.bfloat16)
    return jnp.einsum("nrj,nrc->njc", chosen, mixed, preferred_element_type=jnp.float32)


def collect(total, source_table, sources, targets, picked, live, trimmed, weights):
    edge_total = sources.shape[0]
    block_size = math.gcd(128, edge_total)

    def advance(running, position):
        first_edge = position * block_size
        live_mask = (first_edge + jnp.arange(block_size, dtype=jnp.int32) < live).astype(
            jnp.float32
        )
        chosen = jnp.transpose(trimmed[:, :, picked], (2, 0, 1))
        result = conv_messages(source_table[sources], chosen, weights[0], weights[1], weights[2])
        result = result * live_mask[:, None, None]
        running = running.at[targets].add(result.reshape(block_size, -1))
        return (running, None)

    total, _ = lax.scan(advance, total, jnp.arange(edge_total // block_size, dtype=jnp.int32))
    return total


def fold_sides(padded, axis_dim):
    lower = lax.slice_in_dim(padded, 0, 1, axis=axis_dim)
    middle = lax.slice_in_dim(padded, 2, 3, axis=axis_dim)
    upper = lax.slice_in_dim(padded, 4, 5, axis=axis_dim)
    return lower + middle + upper


def fold_x(partial_value):
    padded = extended(partial_value.astype(jnp.bfloat16), (("gx", 0),), 1).astype(
        partial_value.dtype
    )
    return fold_sides(padded, 0)


def fold_y(partial_value):
    padded = extended(partial_value.astype(jnp.bfloat16), (("gy", 1),), 1).astype(
        partial_value.dtype
    )
    return fold_sides(padded, 1)


def fold_z(partial_value):
    padded = extended(partial_value.astype(jnp.bfloat16), (("gz", 2),), 1).astype(
        partial_value.dtype
    )
    return fold_sides(padded, 2)


def shards(
    features,
    border_atoms,
    inner_source,
    inner_target,
    inner_rotation,
    inner_count,
    cross_source,
    cross_target,
    cross_rotation,
    cross_count,
    rotations,
    order_zero,
    order_one,
    order_two,
):
    full_zero, full_one, full_two = (
        lax.all_gather(order_zero, ("gy", "gz"), axis=0, tiled=True),
        lax.all_gather(order_one, ("gy", "gz"), axis=1, tiled=True),
        lax.all_gather(order_two, ("gy", "gz"), axis=1, tiled=True),
    )
    weights = (full_zero, full_one, full_two)
    local_atoms = features[0, 0, 0]
    atom_total = local_atoms.shape[0]
    harmonics = local_atoms.shape[1]
    channels = local_atoms.shape[2]
    border_rows = border_atoms[0, 0, 0]
    border_total = border_rows.shape[0]
    border = local_atoms[border_rows].reshape(1, 1, 1, border_total, harmonics, channels)
    beside_all = extended(border, (("gx", 0), ("gy", 1), ("gz", 2)), 1)
    beside_all = beside_all.reshape(27 * border_total, harmonics, channels)
    trimmed = rotations[jnp.asarray(kept_rows(LMAX)), :, :]
    gathered = jnp.zeros((atom_total, harmonics * channels), jnp.float32)
    gathered = collect(
        gathered,
        local_atoms,
        inner_source[0, 0, 0],
        inner_target[0, 0, 0],
        inner_rotation[0, 0, 0],
        inner_count[0, 0, 0],
        trimmed,
        weights,
    )
    gathered = collect(
        gathered,
        beside_all,
        cross_source[0, 0, 0],
        cross_target[0, 0, 0],
        cross_rotation[0, 0, 0, 0],
        cross_count[0, 0, 0],
        trimmed,
        weights,
    )
    returned = jnp.zeros((27 * border_total, harmonics * channels), jnp.float32)
    returned = collect(
        returned,
        local_atoms,
        cross_target[0, 0, 0],
        cross_source[0, 0, 0],
        cross_rotation[0, 0, 0, 1],
        cross_count[0, 0, 0],
        trimmed,
        weights,
    )
    returned = returned.reshape(3, 3, 3, border_total, harmonics * channels)
    returned = fold_z(fold_y(fold_x(returned)))
    gathered = gathered.at[border_rows].add(returned.reshape(border_total, -1))
    updated = local_atoms.astype(jnp.float32) + 0.25 * gathered.reshape(
        atom_total, harmonics, channels
    )
    return updated.astype(jnp.bfloat16).reshape(features.shape)


def solution(mesh):
    in_specs = (
        P("gx", "gy", "gz", None, None, None),
        P("gx", "gy", "gz", None),
        P("gx", "gy", "gz", None),
        P("gx", "gy", "gz", None),
        P("gx", "gy", "gz", None),
        P("gx", "gy", "gz"),
        P("gx", "gy", "gz", None),
        P("gx", "gy", "gz", None),
        P("gx", "gy", "gz", None, None),
        P("gx", "gy", "gz"),
        P(),
        P(("gy", "gz"), None),
        P(None, ("gy", "gz"), None),
        P(None, ("gy", "gz"), None),
    )
    out_specs = P("gx", "gy", "gz", None, None, None)
    return jax.shard_map(shards, mesh=mesh, in_specs=in_specs, out_specs=out_specs, check_vma=False)
```

profile of v0, /device:TPU:129, one launch (start us, length us, event | category | flops | bytes accessed | tf_op | source)
XLA Modules:
  0.0 741.7 jit_solution(9208425399380260902)
XLA Ops:
  11.1 5.1 collective-permute-start.1
  21.5 4.1 copy.200
  30.1 2.5 convolution_convert_fusion
  43.0 2.9 collective-permute-start.3
  45.9 6.9 collective-permute-start.2
  57.1 6.1 collective-permute-start.5
  63.2 2.4 collective-permute-start.4
  79.2 7.3 collective-permute-done.4
  95.7 105.9 %all-gather.9.cloned.1.call-done = bf16[64,14,896]{2,1,0:T(8,128)(2,1)} async-done(((bf16[1,14,896]{2,1,0:T(8,128)(2,1)}), bf16[64,14,896]{2,1,0:T(8,128)(2,1)}) %all-gather.9.cloned.1.call-update) | async-done | bytes 1605648 | tf_op jit(solution)/shard_map/all_gather | solution.py:135
  201.6 3.7 reshape.612
  205.3 2.9 copy.203
  212.2 184.6 %all-gather.7.cloned.1.call-done = bf16[2,640,640]{2,0,1:T(2,128)(2,1)} async-done(((bf16[2,10,640]{2,0,1:T(2,128)(2,1)}), bf16[2,640,640]{2,0,1:T(2,128)(2,1)}) %all-gather.7.cloned.1.call-update) | async-done | bytes 1638416 | tf_op jit(solution)/shard_map/all_gather | solution.py:137
  396.8 4.8 fusion.53
  411.9 177.2 %all-gather.5.cloned.1.call-done = bf16[2,768,768]{2,0,1:T(2,128)(2,1)} async-done(((bf16[2,12,768]{2,0,1:T(2,128)(2,1)}), bf16[2,768,768]{2,0,1:T(2,128)(2,1)}) %all-gather.5.cloned.1.call-update) | async-done | bytes 2359312 | tf_op jit(solution)/shard_map/all_gather | solution.py:136
  589.1 6.4 fusion.52
  606.6 4.6 convolution_multiply_fusion
  611.2 4.7 copy.260
  615.9 4.9 copy.261
  620.8 7.5 %scatter_custom_fusion.2 = f32[108,6272]{1,0:T(8,128)} fusion(s32[128]{0:T(128)S(1)} %fusion.50, f32[128,6272]{1,0:T(8,128)} %copy.261, f32[]{:T(128)} %constant.37.clone.1), kind=kCustom, calls=%fused_computation.19 | custom fusion | flops 802816 | bytes 2710016 | tf_op jit(solution)/shard_map/while/body/eval_jaxpr/scatter-add | solution.py:83
  632.3 3.5 convert_element_type.88
  650.7 4.6 collective-permute-start.7
  661.8 4.4 convolution_multiply_fusion.1
  668.0 11.9 %collective-permute-start.8 = (bf16[1,1,3,4,6272]{4,3,2,1,0:T(4,128)(2,1)S(1)}, bf16[1,1,3,4,6272]{4,3,2,1,0:T(4,128)(2,1)S(1)}, u32[]{:S(2)}, u32[]{:S(2)}) collective-permute-start(bf16[1,1,3,4,6272]{4,3,2,1,0:T(4,128)(2,1)S(1)} %get-tuple-element.98), channel_id=1, source_target_pairs={{0,8},{8,16},{16,24},{24,32},{32,40},{40,48},{48,56},{56,0},{1,9},... | collective-permute-start | bytes 451592 | tf_op jit(solution)/shard_map/ppermute | solution.py:17
  682.4 7.7 %collective-permute-done.9 = bf16[1,1,3,4,6272]{4,3,2,1,0:T(4,128)(2,1)S(1)} collective-permute-done((bf16[1,1,3,4,6272]{4,3,2,1,0:T(4,128)(2,1)S(1)}, bf16[1,1,3,4,6272]{4,3,2,1,0:T(4,128)(2,1)S(1)}, u32[]{:S(2)}, u32[]{:S(2)}) %collective-permute-start.9) | collective-permute-done | bytes 150560 | tf_op jit(solution)/shard_map/ppermute | solution.py:20
  692.4 5.5 collective-permute-start.11
  697.8 3.2 convolution_multiply_fusion.2
  701.0 4.5 copy.222
  705.5 4.9 copy.223
  710.3 4.5 copy.242
  714.8 4.9 copy.243
  719.7 6.0 scatter_custom_fusion
  725.7 6.3 scatter_fusion
  (223 shorter events, 110.1 us)
Async XLA Ops:
  6.5 14.4 %copy-start = (bf16[49,49,256]{2,1,0:T(8,128)(2,1)S(1)}, bf16[49,49,256]{2,1,0:T(8,128)(2,1)}, u32[]{:S(2)}) copy-start(bf16[49,49,256]{2,1,0:T(8,128)(2,1)} %param.25) | copy-start | bytes 3687940
  6.5 195.0 %all-gather.9.cloned.1.call-start = ((), (), s32[]{:S(2)}) async-start(), calls=%async_computation.2 | async-start | bytes 1863680 | tf_op jit(solution)/shard_map/all_gather | solution.py:135
  7.3 389.5 %all-gather.7.cloned.1.call-start = ((), (), s32[]{:S(2)}) async-start(), calls=%async_computation.1 | async-start | bytes 1664000 | tf_op jit(solution)/shard_map/all_gather | solution.py:137
  8.0 581.1 %all-gather.5.cloned.1.call-start = ((), (), s32[]{:S(2)}) async-start(), calls=%async_computation | async-start | bytes 2396160 | tf_op jit(solution)/shard_map/all_gather | solution.py:136
  11.1 31.9 %collective-permute-start.1 = (bf16[1,1,1,4,49,128]{5,4,3,2,1,0:T(8,128)(2,1)S(1)}, bf16[1,1,1,4,49,128]{5,4,3,2,1,0:T(8,128)(2,1)S(1)}, u32[]{:S(2)}, u32[]{:S(2)}) collective-permute-start(bf16[1,1,1,4,49,128]{5,4,3,2,1,0:T(8,128)(2,1)S(1)} %bitcast.192), channel_id=1, source_target_pairs={{64,0},{128,64},{192,128},{256,192},{320,256},{384,320},{448,384},... | collective-permute-start | bytes 150536 | tf_op jit(solution)/shard_map/ppermute | solution.py:20
  16.2 26.8 %collective-permute-start = (bf16[1,1,1,4,49,128]{5,4,3,2,1,0:T(8,128)(2,1)S(1)}, bf16[1,1,1,4,49,128]{5,4,3,2,1,0:T(8,128)(2,1)S(1)}, u32[]{:S(2)}, u32[]{:S(2)}) collective-permute-start(bf16[1,1,1,4,49,128]{5,4,3,2,1,0:T(8,128)(2,1)S(1)} %bitcast.193), channel_id=1, source_target_pairs={{0,64},{64,128},{128,192},{192,256},{256,320},{320,384},{384,448},... | collective-permute-start | bytes 150536 | tf_op jit(solution)/shard_map/ppermute | solution.py:17
  41.0 24.7 %copy-start.9 = (bf16[128,29,128]{2,1,0:T(8,128)(2,1)}, bf16[128,29,128]{2,1,0:T(8,128)(2,1)S(1)}, u32[]{:S(2)}) copy-start(bf16[128,29,128]{2,1,0:T(8,128)(2,1)S(1)} %convolution_convert_fusion.2) | copy-start | bytes 2850820
  41.0 11.8 %copy-start.35 = (s32[1,1,1,128]{3,2,1,0:T(1,128)S(1)}, s32[1,1,1,128]{3,2,1,0:T(1,128)}, u32[]{:S(2)}) copy-start(s32[1,1,1,128]{3,2,1,0:T(1,128)} %param.21) | copy-start | bytes 1540
  43.0 22.7 %copy-start.33 = (bf16[1,1,1,4,49,128]{5,4,3,2,1,0:T(8,128)(2,1)}, bf16[1,1,1,4,49,128]{5,4,3,2,1,0:T(8,128)(2,1)S(1)}, u32[]{:S(2)}) copy-start(bf16[1,1,1,4,49,128]{5,4,3,2,1,0:T(8,128)(2,1)S(1)} %collective-permute-done.1) | copy-start | bytes 150532
  43.0 22.7 %copy-start.34 = (bf16[1,1,1,4,49,128]{5,4,3,2,1,0:T(8,128)(2,1)}, bf16[1,1,1,4,49,128]{5,4,3,2,1,0:T(8,128)(2,1)S(1)}, u32[]{:S(2)}) copy-start(bf16[1,1,1,4,49,128]{5,4,3,2,1,0:T(8,128)(2,1)S(1)} %collective-permute-done) | copy-start | bytes 150532
  43.0 12.1 %collective-permute-start.3 = (bf16[3,1,1,4,49,128]{5,4,3,2,1,0:T(8,128)(2,1)S(1)}, bf16[3,1,1,4,49,128]{5,4,3,2,1,0:T(8,128)(2,1)S(1)}, u32[]{:S(2)}, u32[]{:S(2)}) collective-permute-start(bf16[3,1,1,4,49,128]{5,4,3,2,1,0:T(8,128)(2,1)S(1)} %pad_maximum_fusion.4), channel_id=1, source_target_pairs={{8,0},{16,8},{24,16},{32,24},{40,32},{48,40},{56,48},{0,56},{9,1},... | collective-permute-start | bytes 451592 | tf_op jit(solution)/shard_map/ppermute | solution.py:20
  45.9 10.3 %collective-permute-start.2 = (bf16[3,1,1,4,49,128]{5,4,3,2,1,0:T(8,128)(2,1)S(1)}, bf16[3,1,1,4,49,128]{5,4,3,2,1,0:T(8,128)(2,1)S(1)}, u32[]{:S(2)}, u32[]{:S(2)}) collective-permute-start(bf16[3,1,1,4,49,128]{5,4,3,2,1,0:T(8,128)(2,1)S(1)} %pad_maximum_fusion.4), channel_id=1, source_target_pairs={{0,8},{8,16},{16,24},{24,32},{32,40},{40,48},{48,56},{56,0},{1,9},... | collective-permute-start | bytes 451592 | tf_op jit(solution)/shard_map/ppermute | solution.py:17
  55.1 12.0 %copy-start.27 = (bf16[3,1,1,4,49,128]{5,4,3,2,1,0:T(8,128)(2,1)}, bf16[3,1,1,4,49,128]{5,4,3,2,1,0:T(8,128)(2,1)S(1)}, u32[]{:S(2)}) copy-start(bf16[3,1,1,4,49,128]{5,4,3,2,1,0:T(8,128)(2,1)S(1)} %collective-permute-done.3) | copy-start | bytes 451588
  56.2 9.4 %copy-start.28 = (bf16[3,1,1,4,49,128]{5,4,3,2,1,0:T(8,128)(2,1)}, bf16[3,1,1,4,49,128]{5,4,3,2,1,0:T(8,128)(2,1)S(1)}, u32[]{:S(2)}) copy-start(bf16[3,1,1,4,49,128]{5,4,3,2,1,0:T(8,128)(2,1)S(1)} %collective-permute-done.2) | copy-start | bytes 451588
  57.1 22.1 %collective-permute-start.5 = (bf16[3,3,1,4,49,128]{5,4,3,2,1,0:T(8,128)(2,1)}, bf16[3,3,1,4,49,128]{5,4,3,2,1,0:T(8,128)(2,1)}, u32[]{:S(2)}, u32[]{:S(2)}) collective-permute-start(bf16[3,3,1,4,49,128]{5,4,3,2,1,0:T(8,128)(2,1)} %pad_maximum_fusion.1), channel_id=1, source_target_pairs={{1,0},{2,1},{3,2},{4,3},{5,4},{6,5},{7,6},{0,7},{9,8},{10,9},{11,1... | collective-permute-start | bytes 1354760 | tf_op jit(solution)/shard_map/ppermute | solution.py:20
  63.2 23.3 %collective-permute-start.4 = (bf16[3,3,1,4,49,128]{5,4,3,2,1,0:T(8,128)(2,1)}, bf16[3,3,1,4,49,128]{5,4,3,2,1,0:T(8,128)(2,1)}, u32[]{:S(2)}, u32[]{:S(2)}) collective-permute-start(bf16[3,3,1,4,49,128]{5,4,3,2,1,0:T(8,128)(2,1)} %pad_maximum_fusion.1), channel_id=1, source_target_pairs={{0,1},{1,2},{2,3},{3,4},{4,5},{5,6},{6,7},{7,0},{8,9},{9,10},{10,1... | collective-permute-start | bytes 1354760 | tf_op jit(solution)/shard_map/ppermute | solution.py:17
  65.8 10.3 %slice-start = ((bf16[128,29,128]{2,1,0:T(8,128)(2,1)}), bf16[128,7,128]{2,1,0:T(8,128)(2,1)S(1)}, s32[]{:S(2)}) async-start(bf16[128,29,128]{2,1,0:T(8,128)(2,1)} %copy-done.9), calls=%async_computation.3 | async-start | bytes 524288 | tf_op jit(solution)/shard_map/while/body/eval_jaxpr/slice | solution.py:41
  67.1 9.9 %copy-start.22 = (bf16[128,5,128]{2,1,0:T(8,128)(2,1)S(1)}, bf16[128,5,128]{2,1,0:T(8,128)(2,1)}, u32[]{:S(2)}) copy-start(bf16[128,5,128]{2,1,0:T(8,128)(2,1)} %get-tuple-element.94) | copy-start | bytes 491524
  69.5 20.6 %copy-start.5 = (bf16[128,29,49]{2,1,0:T(8,128)(2,1)}, bf16[128,29,49]{2,1,0:T(8,128)(2,1)S(1)}, u32[]{:S(2)}) copy-start(bf16[128,29,49]{2,1,0:T(8,128)(2,1)S(1)} %gather_fusion.3) | copy-start | bytes 1091332
  649.1 9.9 %copy-start.32 = (bf16[128,5,128]{2,0,1:T(8,128)(2,1)S(1)}, bf16[128,5,128]{2,0,1:T(8,128)(2,1)}, u32[]{:S(2)}) copy-start(bf16[128,5,128]{2,0,1:T(8,128)(2,1)} %copy.239) | copy-start | bytes 491524
  650.4 10.7 %copy-start.30 = (bf16[128,5,128]{2,0,1:T(8,128)(2,1)S(1)}, bf16[128,5,128]{2,0,1:T(8,128)(2,1)}, u32[]{:S(2)}) copy-start(bf16[128,5,128]{2,0,1:T(8,128)(2,1)} %copy.240) | copy-start | bytes 491524
  650.4 11.4 %copy-start.6 = (bf16[128,29,49]{2,1,0:T(8,128)(2,1)S(1)}, bf16[128,29,49]{2,1,0:T(8,128)(2,1)}, u32[]{:S(2)}) copy-start(bf16[128,29,49]{2,1,0:T(8,128)(2,1)} %copy-done.5) | copy-start | bytes 1091332
  650.7 15.5 %collective-permute-start.7 = (bf16[1,3,3,4,6272]{4,3,2,1,0:T(4,128)(2,1)S(1)}, bf16[1,3,3,4,6272]{4,3,2,1,0:T(4,128)(2,1)S(1)}, u32[]{:S(2)}, u32[]{:S(2)}) collective-permute-start(bf16[1,3,3,4,6272]{4,3,2,1,0:T(4,128)(2,1)S(1)} %slice.185), channel_id=1, source_target_pairs={{64,0},{128,64},{192,128},{256,192},{320,256},{384,320},{448,384},... | collective-permute-start | bytes 1354760 | tf_op jit(solution)/shard_map/ppermute | solution.py:20
  655.3 11.6 %collective-permute-start.6 = (bf16[1,3,3,4,6272]{4,3,2,1,0:T(4,128)(2,1)}, bf16[1,3,3,4,6272]{4,3,2,1,0:T(4,128)(2,1)S(1)}, u32[]{:S(2)}, u32[]{:S(2)}) collective-permute-start(bf16[1,3,3,4,6272]{4,3,2,1,0:T(4,128)(2,1)} %slice.183), channel_id=1, source_target_pairs={{0,64},{64,128},{128,192},{192,256},{256,320},{320,384},{384,448},... | collective-permute-start | bytes 1354760 | tf_op jit(solution)/shard_map/ppermute | solution.py:17
  666.2 15.7 %copy-start.14 = (bf16[128,29,128]{2,0,1:T(8,128)(2,1)S(1)}, bf16[128,29,128]{2,0,1:T(8,128)(2,1)}, u32[]{:S(2)}) copy-start(bf16[128,29,128]{2,0,1:T(8,128)(2,1)} %constant_dynamic-update-slice_fusion.2) | copy-start | bytes 2850820
  666.2 15.7 %copy-start.31 = (bf16[128,5,128]{2,0,1:T(8,128)(2,1)S(1)}, bf16[128,5,128]{2,0,1:T(8,128)(2,1)}, u32[]{:S(2)}) copy-start(bf16[128,5,128]{2,0,1:T(8,128)(2,1)} %copy.219) | copy-start | bytes 491524
  666.2 15.7 %copy-start.29 = (bf16[128,5,128]{2,0,1:T(8,128)(2,1)S(1)}, bf16[128,5,128]{2,0,1:T(8,128)(2,1)}, u32[]{:S(2)}) copy-start(bf16[128,5,128]{2,0,1:T(8,128)(2,1)} %copy.220) | copy-start | bytes 491524
  667.8 30.0 %copy-start.4 = (bf16[128,29,49]{2,1,0:T(8,128)(2,1)S(1)}, bf16[128,29,49]{2,1,0:T(8,128)(2,1)}, u32[]{:S(2)}) copy-start(bf16[128,29,49]{2,1,0:T(8,128)(2,1)} %copy-done.3) | copy-start | bytes 1091332
  668.0 14.4 %collective-permute-start.8 = (bf16[1,1,3,4,6272]{4,3,2,1,0:T(4,128)(2,1)S(1)}, bf16[1,1,3,4,6272]{4,3,2,1,0:T(4,128)(2,1)S(1)}, u32[]{:S(2)}, u32[]{:S(2)}) collective-permute-start(bf16[1,1,3,4,6272]{4,3,2,1,0:T(4,128)(2,1)S(1)} %get-tuple-element.98), channel_id=1, source_target_pairs={{0,8},{8,16},{16,24},{24,32},{32,40},{40,48},{48,56},{56,0},{1,9},... | collective-permute-start | bytes 451592 | tf_op jit(solution)/shard_map/ppermute | solution.py:17
  679.9 10.2 %collective-permute-start.9 = (bf16[1,1,3,4,6272]{4,3,2,1,0:T(4,128)(2,1)S(1)}, bf16[1,1,3,4,6272]{4,3,2,1,0:T(4,128)(2,1)S(1)}, u32[]{:S(2)}, u32[]{:S(2)}) collective-permute-start(bf16[1,1,3,4,6272]{4,3,2,1,0:T(4,128)(2,1)S(1)} %get-tuple-element.110), channel_id=1, source_target_pairs={{8,0},{16,8},{24,16},{32,24},{40,32},{48,40},{56,48},{0,56},{9,1},... | collective-permute-start | bytes 451592 | tf_op jit(solution)/shard_map/ppermute | solution.py:20
  690.4 41.5 %collective-permute-start.10 = (bf16[1,1,1,4,6272]{4,3,2,1,0:T(4,128)(2,1)S(1)}, bf16[1,1,1,4,6272]{4,3,2,1,0:T(4,128)(2,1)S(1)}, u32[]{:S(2)}, u32[]{:S(2)}) collective-permute-start(bf16[1,1,1,4,6272]{4,3,2,1,0:T(4,128)(2,1)S(1)} %get-tuple-element.111), channel_id=1, source_target_pairs={{0,1},{1,2},{2,3},{3,4},{4,5},{5,6},{6,7},{7,0},{8,9},{9,10},{10,1... | collective-permute-start | bytes 150536 | tf_op jit(solution)/shard_map/ppermute | solution.py:17
  692.4 39.6 %collective-permute-start.11 = (bf16[1,1,1,4,6272]{4,3,2,1,0:T(4,128)(2,1)S(1)}, bf16[1,1,1,4,6272]{4,3,2,1,0:T(4,128)(2,1)S(1)}, u32[]{:S(2)}, u32[]{:S(2)}) collective-permute-start(bf16[1,1,1,4,6272]{4,3,2,1,0:T(4,128)(2,1)S(1)} %get-tuple-element.112), channel_id=1, source_target_pairs={{1,0},{2,1},{3,2},{4,3},{5,4},{6,5},{7,6},{0,7},{9,8},{10,9},{11,1... | collective-permute-start | bytes 150536 | tf_op jit(solution)/shard_map/ppermute | solution.py:20
  (21 other events, 65.0 us)
Sparse Core Ops, SparseCore 0:
  9.5 192.0 all-gather.8
  203.7 193.0 all-gather.6
  398.9 190.2 all-gather.4
where the time goes:
time: 748 us; the launch traced here: 742 us
  waiting for transfers between devices  489 us (65%)
  local copies, waits for them, and re-layouts  116 us (16%)
  starting transfers between devices  53.6 us (7%)
  matrix products  36.7 us (5%)
  other arithmetic  31.6 us (4%)
  between operations  15.5 us (2%)
    all_gather x1, waiting for transfers between devices, shards(): lax.all_gather(order_two, ('gy', 'gz'), axis=1, tiled=True)  185 us
    all_gather x1, waiting for transfers between devices, shards(): lax.all_gather(order_one, ('gy', 'gz'), axis=1, tiled=True)  177 us
    all_gather x1, waiting for transfers between devices, shards(): lax.all_gather(order_zero, ('gy', 'gz'), axis=0, tiled=True)  106 us
    ppermute x6, starting transfers between devices, extended(): lax.ppermute(lax.slice_in_dim(block, block.shape[dim] - width, None, axis...  27.5 us
    ppermute x6, starting transfers between devices, extended(): lax.ppermute(lax.slice_in_dim(block, 0, width, axis=dim), axis, backward)  26 us
    scatter-add x3, other arithmetic, advance(): running = running.at[targets].add(result.reshape(block_size, -1))  19.8 us
  transfers between devices with their start and end apart: 15, of which 9 were waited for; matrix products, arithmetic and copies ran while one was open for 16% of the time, Pallas kernels for 0%

commit v1 on v0

--- a/solution.py
+++ b/solution.py
@@ -134,7 +134,12 @@
     full_zero, full_one, full_two = (
         lax.all_gather(order_zero, ("gy", "gz"), axis=0, tiled=True),
         lax.all_gather(order_one, ("gy", "gz"), axis=1, tiled=True),
-        lax.all_gather(order_two, ("gy", "gz"), axis=1, tiled=True),
+        jnp.concatenate(
+            lax.all_to_all(
+                jnp.stack([order_two] * lax.axis_size(("gy", "gz"))), ("gy", "gz"), 0, 0
+            ),
+            axis=1,
+        ),
     )
     weights = (full_zero, full_one, full_two)
     local_atoms = features[0, 0, 0]

time: 748 us -> 574 us (0.77)
  waiting for transfers between devices: 489 us -> 281 us
  local copies, waits for them, and re-layouts: 116 us -> 133 us
  starting transfers between devices: 53.6 us -> 63.1 us
    all_gather x1 -> x0, waiting for transfers between devices: 185 us -> none  [shards(): lax.all_gather(order_two, ('gy', 'gz'), axis=1, tiled=True)]
    all_gather x1, waiting for transfers between devices: 106 us -> 91.6 us  [shards(): lax.all_gather(order_zero, ('gy', 'gz'), axis=0, tiled=True)]
    all_gather x1, waiting for transfers between devices: 177 us -> 163 us  [shards(): lax.all_gather(order_one, ('gy', 'gz'), axis=1, tiled=True)]
    all_to_all x0 -> x1, starting transfers between devices: none -> 12.8 us  [shards(): lax.all_to_all(jnp.stack([order_two] * lax.axis_size(('gy', 'gz'))), ('gy...]
    ppermute x6, waiting for transfers between devices: 9.93 us -> 18.5 us  [extended(): lax.ppermute(lax.slice_in_dim(block, 0, width, axis=dim), axis, backward)]
    unnamed x85 -> x101, local copies, waits for them, and re-layouts: 14.5 us -> 17.6 us
  transfers between devices with their start and end apart: 15 -> 15, of which waited for: 9 -> 7; matrix products, arithmetic and copies ran while one was open for 16% -> 23% of each run, Pallas kernels for 0% -> 0%
where the time goes in v1:
time: 574 us; the launch traced here: 563 us
  waiting for transfers between devices  281 us (49%)
  local copies, waits for them, and re-layouts  133 us (23%)
  starting transfers between devices  63.1 us (11%)
  matrix products  39.7 us (7%)
  other arithmetic  30.7 us (5%)
  between operations  15.9 us (3%)
    all_gather x1, waiting for transfers between devices, shards(): lax.all_gather(order_one, ('gy', 'gz'), axis=1, tiled=True)  163 us
    all_gather x1, waiting for transfers between devices, shards(): lax.all_gather(order_zero, ('gy', 'gz'), axis=0, tiled=True)  91.6 us
    ppermute x6, starting transfers between devices, extended(): lax.ppermute(lax.slice_in_dim(block, 0, width, axis=dim), axis, backward)  25.2 us
    ppermute x6, starting transfers between devices, extended(): lax.ppermute(lax.slice_in_dim(block, block.shape[dim] - width, None, axis...  25.1 us
    scatter-add x3, other arithmetic, advance(): running = running.at[targets].add(result.reshape(block_size, -1))  19.6 us
    ppermute x6, waiting for transfers between devices, extended(): lax.ppermute(lax.slice_in_dim(block, 0, width, axis=dim), axis, backward)  18.5 us
    unnamed x101, local copies, waits for them, and re-layouts  17.6 us
    all_to_all x1, starting transfers between devices, shards(): lax.all_to_all(jnp.stack([order_two] * lax.axis_size(('gy', 'gz'))), ('gy...  12.8 us
  transfers between devices with their start and end apart: 15, of which 7 were waited for; matrix products, arithmetic and copies ran while one was open for 23% of the time, Pallas kernels for 0%

profile of v1, /device:TPU:129, one launch (start us, length us, event | category | flops | bytes accessed | tf_op | source)
XLA Modules:
  0.0 563.4 jit_solution(1091475274353131737)
XLA Ops:
  10.9 5.1 collective-permute-start.1
  18.0 2.8 stack.2
  20.7 12.8 %all-to-all-start = ((bf16[64,2,10,640]{3,1,2,0:T(2,128)(2,1)}), bf16[64,2,10,640]{3,1,2,0:T(2,128)(2,1)S(1)}, u32[]{:S(2)}, u32[]{:S(2)}) async-start(bf16[64,2,10,640]{3,1,2,0:T(2,128)(2,1)} %stack.2), calls=%async_computation | async-start | bytes 3276800 | tf_op jit(solution)/shard_map/all_to_all | solution.py:138
  35.9 5.1 copy.199
  61.0 5.4 collective-permute-start.2
  66.5 10.8 %collective-permute-done.3 = bf16[3,1,1,4,49,128]{5,4,3,2,1,0:T(8,128)(2,1)S(1)} collective-permute-done((bf16[3,1,1,4,49,128]{5,4,3,2,1,0:T(8,128)(2,1)S(1)}, bf16[3,1,1,4,49,128]{5,4,3,2,1,0:T(8,128)(2,1)S(1)}, u32[]{:S(2)}, u32[]{:S(2)}) %collective-permute-start.3) | collective-permute-done | bytes 150560 | tf_op jit(solution)/shard_map/ppermute | solution.py:20
  79.8 5.8 %collective-permute-start.5 = (bf16[3,3,1,4,49,128]{5,4,3,2,1,0:T(8,128)(2,1)}, bf16[3,3,1,4,49,128]{5,4,3,2,1,0:T(8,128)(2,1)}, u32[]{:S(2)}, u32[]{:S(2)}) collective-permute-start(bf16[3,3,1,4,49,128]{5,4,3,2,1,0:T(8,128)(2,1)} %pad_maximum_fusion.1), channel_id=1, source_target_pairs={{1,0},{2,1},{3,2},{4,3},{5,4},{6,5},{7,6},{0,7},{9,8},{10,9},{11,1... | collective-permute-start | bytes 1354760 | tf_op jit(solution)/shard_map/ppermute | solution.py:20
  89.0 3.3 gather_fusion.3
  102.9 5.4 collective-permute-done.4
  119.0 91.6 %all-gather.6.cloned.1.call-done = bf16[64,14,896]{2,1,0:T(8,128)(2,1)} async-done(((bf16[1,14,896]{2,1,0:T(8,128)(2,1)}), bf16[64,14,896]{2,1,0:T(8,128)(2,1)}) %all-gather.6.cloned.1.call-update) | async-done | bytes 1605648 | tf_op jit(solution)/shard_map/all_gather | solution.py:135
  210.6 3.8 reshape.623
  214.4 2.9 copy.202
  222.3 9.3 %slice_reduce_fusion = (bf16[64,10,640]{2,1,0:T(8,128)(2,1)}, bf16[64,10,640]{2,1,0:T(8,128)(2,1)}) fusion(bf16[2,64,10,640]{3,0,2,1:T(2,128)(2,1)S(1)} %bitcast.157), kind=kLoop, calls=%fused_computation.15 | loop fusion | bytes 3276800 | tf_op jit(solution)/shard_map/while/body/eval_jaxpr/slice | solution.py:59
  243.9 163.5 %all-gather.4.cloned.1.call-done = bf16[2,768,768]{2,0,1:T(2,128)(2,1)} async-done(((bf16[2,12,768]{2,0,1:T(2,128)(2,1)}), bf16[2,768,768]{2,0,1:T(2,128)(2,1)}) %all-gather.4.cloned.1.call-update) | async-done | bytes 2359312 | tf_op jit(solution)/shard_map/all_gather | solution.py:136
  407.4 6.4 %fusion.52 = (bf16[1,768,768]{2,0,1:T(2,128)(2,1)S(1)}, bf16[1,768,768]{2,0,1:T(2,128)(2,1)S(1)}) fusion(bf16[2,768,768]{2,0,1:T(2,128)(2,1)} %all-gather.4.cloned.1.call-done), kind=kLoop, calls=%fused_computation.133 | loop fusion | bytes 4718592 | tf_op jit(solution)/shard_map/while/body/eval_jaxpr/slice | solution.py:53
  429.8 4.3 convolution_multiply_fusion
  434.0 4.5 copy.257
  438.5 5.3 copy.258
  443.8 7.5 %scatter_custom_fusion.2 = f32[108,6272]{1,0:T(8,128)} fusion(s32[128]{0:T(128)S(1)} %fusion.50, f32[128,6272]{1,0:T(8,128)} %copy.258, f32[]{:T(128)} %constant.37.clone.1), kind=kCustom, calls=%fused_computation.21 | custom fusion | flops 802816 | bytes 2710016 | tf_op jit(solution)/shard_map/while/body/eval_jaxpr/scatter-add | solution.py:83
  454.5 3.5 convert_element_type.88
  477.4 4.4 collective-permute-start.7
  488.4 4.4 convolution_multiply_fusion.1
  494.4 11.9 %collective-permute-start.8 = (bf16[1,1,3,4,6272]{4,3,2,1,0:T(4,128)(2,1)S(1)}, bf16[1,1,3,4,6272]{4,3,2,1,0:T(4,128)(2,1)S(1)}, u32[]{:S(2)}, u32[]{:S(2)}) collective-permute-start(bf16[1,1,3,4,6272]{4,3,2,1,0:T(4,128)(2,1)S(1)} %get-tuple-element.98), channel_id=1, source_target_pairs={{0,8},{8,16},{16,24},{24,32},{32,40},{40,48},{48,56},{56,0},{1,9},... | collective-permute-start | bytes 451592 | tf_op jit(solution)/shard_map/ppermute | solution.py:17
  508.9 7.7 %collective-permute-done.9 = bf16[1,1,3,4,6272]{4,3,2,1,0:T(4,128)(2,1)S(1)} collective-permute-done((bf16[1,1,3,4,6272]{4,3,2,1,0:T(4,128)(2,1)S(1)}, bf16[1,1,3,4,6272]{4,3,2,1,0:T(4,128)(2,1)S(1)}, u32[]{:S(2)}, u32[]{:S(2)}) %collective-permute-start.9) | collective-permute-done | bytes 150560 | tf_op jit(solution)/shard_map/ppermute | solution.py:20
  518.9 5.5 collective-permute-start.11
  524.4 3.1 convolution_multiply_fusion.2
  527.5 3.7 copy.219
  531.1 3.1 copy.220
  534.2 3.7 copy.239
  537.9 3.1 copy.240
  541.0 6.0 %scatter_custom_fusion = f32[32,6272]{1,0:T(8,128)S(1)} fusion(s32[128]{0:T(128)S(1)} %fusion.44, f32[128,6272]{1,0:T(8,128)} %copy.220, f32[]{:T(128)} %constant.37.clone.1), kind=kCustom, calls=%fused_computation.68 | custom fusion | flops 802816 | bytes 803328 | tf_op jit(solution)/shard_map/while/body/eval_jaxpr/scatter-add | solution.py:83
  547.0 6.1 %scatter_fusion = f32[32,6272]{1,0:T(8,128)S(1)} fusion(f32[32,6272]{1,0:T(8,128)S(1)} %scatter_custom_fusion, s32[128]{0:T(128)S(1)} %fusion.47, f32[128,6272]{1,0:T(8,128)} %copy.240), kind=kCustom, calls=%fused_computation.9 | custom fusion | flops 802816 | bytes 9634304 | tf_op jit(solution)/shard_map/while/body/eval_jaxpr/scatter-add | solution.py:83
  (241 shorter events, 125.9 us)
Async XLA Ops:
  6.5 27.9 %copy-start = (bf16[49,49,256]{2,1,0:T(8,128)(2,1)S(1)}, bf16[49,49,256]{2,1,0:T(8,128)(2,1)}, u32[]{:S(2)}) copy-start(bf16[49,49,256]{2,1,0:T(8,128)(2,1)} %param.25) | copy-start | bytes 3687940
  6.5 204.1 %all-gather.6.cloned.1.call-start = ((), (), s32[]{:S(2)}) async-start(), calls=%async_computation.2 | async-start | bytes 1863680 | tf_op jit(solution)/shard_map/all_gather | solution.py:135
  10.9 46.9 %collective-permute-start.1 = (bf16[1,1,1,4,49,128]{5,4,3,2,1,0:T(8,128)(2,1)}, bf16[1,1,1,4,49,128]{5,4,3,2,1,0:T(8,128)(2,1)}, u32[]{:S(2)}, u32[]{:S(2)}) collective-permute-start(bf16[1,1,1,4,49,128]{5,4,3,2,1,0:T(8,128)(2,1)} %bitcast.31), channel_id=1, source_target_pairs={{64,0},{128,64},{192,128},{256,192},{320,256},{384,320},{448,384},... | collective-permute-start | bytes 150536 | tf_op jit(solution)/shard_map/ppermute | solution.py:20
  16.0 41.8 %collective-permute-start = (bf16[1,1,1,4,49,128]{5,4,3,2,1,0:T(8,128)(2,1)}, bf16[1,1,1,4,49,128]{5,4,3,2,1,0:T(8,128)(2,1)}, u32[]{:S(2)}, u32[]{:S(2)}) collective-permute-start(bf16[1,1,1,4,49,128]{5,4,3,2,1,0:T(8,128)(2,1)} %bitcast.31), channel_id=1, source_target_pairs={{0,64},{64,128},{128,192},{192,256},{256,320},{320,384},{384,448},... | collective-permute-start | bytes 150536 | tf_op jit(solution)/shard_map/ppermute | solution.py:17
  20.7 13.6 %copy-start.41 = (s32[1,1,1,128]{3,2,1,0:T(1,128)S(1)}, s32[1,1,1,128]{3,2,1,0:T(1,128)}, u32[]{:S(2)}) copy-start(s32[1,1,1,128]{3,2,1,0:T(1,128)} %param.22) | copy-start | bytes 1540
  20.7 13.6 %copy-start.42 = (s32[1,1,1,128]{3,2,1,0:T(1,128)S(1)}, s32[1,1,1,128]{3,2,1,0:T(1,128)}, u32[]{:S(2)}) copy-start(s32[1,1,1,128]{3,2,1,0:T(1,128)} %param.19) | copy-start | bytes 1540
  20.7 13.7 %copy-start.39 = (s32[1,1,1,2,128]{4,3,2,1,0:T(2,128)S(1)}, s32[1,1,1,2,128]{4,3,2,1,0:T(2,128)}, u32[]{:S(2)}) copy-start(s32[1,1,1,2,128]{4,3,2,1,0:T(2,128)} %param.23) | copy-start | bytes 3076
  20.7 13.7 %copy-start.40 = (s32[29]{0:T(128)S(1)}, s32[29]{0:T(128)}, u32[]{:S(2)}) copy-start(s32[29]{0:T(128)} %constant.80) | copy-start | bytes 352
  20.7 201.5 %all-to-all-start = ((bf16[64,2,10,640]{3,1,2,0:T(2,128)(2,1)}), bf16[64,2,10,640]{3,1,2,0:T(2,128)(2,1)S(1)}, u32[]{:S(2)}, u32[]{:S(2)}) async-start(bf16[64,2,10,640]{3,1,2,0:T(2,128)(2,1)} %stack.2), calls=%async_computation | async-start | bytes 3276800 | tf_op jit(solution)/shard_map/all_to_all | solution.py:138
  33.6 373.8 %all-gather.4.cloned.1.call-start = ((), (), s32[]{:S(2)}) async-start(), calls=%async_computation.1 | async-start | bytes 2396160 | tf_op jit(solution)/shard_map/all_gather | solution.py:136
  56.7 30.9 %copy-start.10 = (bf16[128,29,128]{2,1,0:T(8,128)(2,1)}, bf16[128,29,128]{2,1,0:T(8,128)(2,1)S(1)}, u32[]{:S(2)}) copy-start(bf16[128,29,128]{2,1,0:T(8,128)(2,1)S(1)} %convolution_convert_fusion.2) | copy-start | bytes 2850820
  57.8 34.4 %slice-start = ((bf16[128,29,128]{2,1,0:T(8,128)(2,1)}), bf16[128,7,128]{2,1,0:T(8,128)(2,1)S(1)}, s32[]{:S(2)}) async-start(bf16[128,29,128]{2,1,0:T(8,128)(2,1)} %copy-done.9), calls=%async_computation.3 | async-start | bytes 524288 | tf_op jit(solution)/shard_map/while/body/eval_jaxpr/slice | solution.py:41
  58.8 18.6 %collective-permute-start.3 = (bf16[3,1,1,4,49,128]{5,4,3,2,1,0:T(8,128)(2,1)S(1)}, bf16[3,1,1,4,49,128]{5,4,3,2,1,0:T(8,128)(2,1)S(1)}, u32[]{:S(2)}, u32[]{:S(2)}) collective-permute-start(bf16[3,1,1,4,49,128]{5,4,3,2,1,0:T(8,128)(2,1)S(1)} %pad_maximum_fusion.4), channel_id=1, source_target_pairs={{8,0},{16,8},{24,16},{32,24},{40,32},{48,40},{56,48},{0,56},{9,1},... | collective-permute-start | bytes 451592 | tf_op jit(solution)/shard_map/ppermute | solution.py:20
  61.0 16.3 %collective-permute-start.2 = (bf16[3,1,1,4,49,128]{5,4,3,2,1,0:T(8,128)(2,1)S(1)}, bf16[3,1,1,4,49,128]{5,4,3,2,1,0:T(8,128)(2,1)S(1)}, u32[]{:S(2)}, u32[]{:S(2)}) collective-permute-start(bf16[3,1,1,4,49,128]{5,4,3,2,1,0:T(8,128)(2,1)S(1)} %pad_maximum_fusion.4), channel_id=1, source_target_pairs={{0,8},{8,16},{16,24},{24,32},{32,40},{40,48},{48,56},{56,0},{1,9},... | collective-permute-start | bytes 451592 | tf_op jit(solution)/shard_map/ppermute | solution.py:17
  79.8 15.2 %copy-start.25 = (bf16[128,6,128]{2,1,0:T(8,128)(2,1)S(1)}, bf16[128,6,128]{2,1,0:T(8,128)(2,1)}, u32[]{:S(2)}) copy-start(bf16[128,6,128]{2,1,0:T(8,128)(2,1)} %get-tuple-element.88) | copy-start | bytes 589828
  79.8 23.1 %collective-permute-start.5 = (bf16[3,3,1,4,49,128]{5,4,3,2,1,0:T(8,128)(2,1)}, bf16[3,3,1,4,49,128]{5,4,3,2,1,0:T(8,128)(2,1)}, u32[]{:S(2)}, u32[]{:S(2)}) collective-permute-start(bf16[3,3,1,4,49,128]{5,4,3,2,1,0:T(8,128)(2,1)} %pad_maximum_fusion.1), channel_id=1, source_target_pairs={{1,0},{2,1},{3,2},{4,3},{5,4},{6,5},{7,6},{0,7},{9,8},{10,9},{11,1... | collective-permute-start | bytes 1354760 | tf_op jit(solution)/shard_map/ppermute | solution.py:20
  85.6 22.6 %collective-permute-start.4 = (bf16[3,3,1,4,49,128]{5,4,3,2,1,0:T(8,128)(2,1)}, bf16[3,3,1,4,49,128]{5,4,3,2,1,0:T(8,128)(2,1)}, u32[]{:S(2)}, u32[]{:S(2)}) collective-permute-start(bf16[3,3,1,4,49,128]{5,4,3,2,1,0:T(8,128)(2,1)} %pad_maximum_fusion.1), channel_id=1, source_target_pairs={{0,1},{1,2},{2,3},{3,4},{4,5},{5,6},{6,7},{7,0},{8,9},{9,10},{10,1... | collective-permute-start | bytes 1354760 | tf_op jit(solution)/shard_map/ppermute | solution.py:17
  96.7 11.6 %copy-start.33 = (bf16[3,1,1,4,49,128]{5,4,3,2,1,0:T(8,128)(2,1)S(1)}, bf16[3,1,1,4,49,128]{5,4,3,2,1,0:T(8,128)(2,1)}, u32[]{:S(2)}) copy-start(bf16[3,1,1,4,49,128]{5,4,3,2,1,0:T(8,128)(2,1)} %copy-done.32) | copy-start | bytes 451588
  417.6 12.2 %copy-start.7 = (bf16[128,29,49]{2,1,0:T(8,128)(2,1)S(1)}, bf16[128,29,49]{2,1,0:T(8,128)(2,1)}, u32[]{:S(2)}) copy-start(bf16[128,29,49]{2,1,0:T(8,128)(2,1)} %copy-done.6) | copy-start | bytes 1091332
  474.3 11.7 %copy-start.38 = (bf16[128,5,128]{2,0,1:T(8,128)(2,1)S(1)}, bf16[128,5,128]{2,0,1:T(8,128)(2,1)}, u32[]{:S(2)}) copy-start(bf16[128,5,128]{2,0,1:T(8,128)(2,1)} %copy.236) | copy-start | bytes 491524
  474.3 12.4 %copy-start.17 = (bf16[128,29,128]{2,0,1:T(8,128)(2,1)S(1)}, bf16[128,29,128]{2,0,1:T(8,128)(2,1)}, u32[]{:S(2)}) copy-start(bf16[128,29,128]{2,0,1:T(8,128)(2,1)} %fusion.2) | copy-start | bytes 2850820
  476.3 11.4 %copy-start.36 = (bf16[128,5,128]{2,0,1:T(8,128)(2,1)S(1)}, bf16[128,5,128]{2,0,1:T(8,128)(2,1)}, u32[]{:S(2)}) copy-start(bf16[128,5,128]{2,0,1:T(8,128)(2,1)} %copy.237) | copy-start | bytes 491524
  476.3 12.2 %copy-start.5 = (bf16[128,29,49]{2,1,0:T(8,128)(2,1)S(1)}, bf16[128,29,49]{2,1,0:T(8,128)(2,1)}, u32[]{:S(2)}) copy-start(bf16[128,29,49]{2,1,0:T(8,128)(2,1)} %gather_fusion.3) | copy-start | bytes 1091332
  477.4 15.4 %collective-permute-start.7 = (bf16[1,3,3,4,6272]{4,3,2,1,0:T(4,128)(2,1)}, bf16[1,3,3,4,6272]{4,3,2,1,0:T(4,128)(2,1)S(1)}, u32[]{:S(2)}, u32[]{:S(2)}) collective-permute-start(bf16[1,3,3,4,6272]{4,3,2,1,0:T(4,128)(2,1)} %slice.187), channel_id=1, source_target_pairs={{64,0},{128,64},{192,128},{256,192},{320,256},{384,320},{448,384},... | collective-permute-start | bytes 1354760 | tf_op jit(solution)/shard_map/ppermute | solution.py:20
  481.8 11.6 %collective-permute-start.6 = (bf16[1,3,3,4,6272]{4,3,2,1,0:T(4,128)(2,1)}, bf16[1,3,3,4,6272]{4,3,2,1,0:T(4,128)(2,1)S(1)}, u32[]{:S(2)}, u32[]{:S(2)}) collective-permute-start(bf16[1,3,3,4,6272]{4,3,2,1,0:T(4,128)(2,1)} %slice.185), channel_id=1, source_target_pairs={{0,64},{64,128},{128,192},{192,256},{256,320},{320,384},{384,448},... | collective-permute-start | bytes 1354760 | tf_op jit(solution)/shard_map/ppermute | solution.py:17
  492.8 15.7 %copy-start.37 = (bf16[128,5,128]{2,0,1:T(8,128)(2,1)S(1)}, bf16[128,5,128]{2,0,1:T(8,128)(2,1)}, u32[]{:S(2)}) copy-start(bf16[128,5,128]{2,0,1:T(8,128)(2,1)} %copy.216) | copy-start | bytes 491524
  492.8 15.7 %copy-start.35 = (bf16[128,5,128]{2,0,1:T(8,128)(2,1)S(1)}, bf16[128,5,128]{2,0,1:T(8,128)(2,1)}, u32[]{:S(2)}) copy-start(bf16[128,5,128]{2,0,1:T(8,128)(2,1)} %copy.217) | copy-start | bytes 491524
  494.3 30.0 %copy-start.4 = (bf16[128,29,49]{2,1,0:T(8,128)(2,1)S(1)}, bf16[128,29,49]{2,1,0:T(8,128)(2,1)}, u32[]{:S(2)}) copy-start(bf16[128,29,49]{2,1,0:T(8,128)(2,1)} %copy-done.3) | copy-start | bytes 1091332
  494.4 14.5 %collective-permute-start.8 = (bf16[1,1,3,4,6272]{4,3,2,1,0:T(4,128)(2,1)S(1)}, bf16[1,1,3,4,6272]{4,3,2,1,0:T(4,128)(2,1)S(1)}, u32[]{:S(2)}, u32[]{:S(2)}) collective-permute-start(bf16[1,1,3,4,6272]{4,3,2,1,0:T(4,128)(2,1)S(1)} %get-tuple-element.98), channel_id=1, source_target_pairs={{0,8},{8,16},{16,24},{24,32},{32,40},{40,48},{48,56},{56,0},{1,9},... | collective-permute-start | bytes 451592 | tf_op jit(solution)/shard_map/ppermute | solution.py:17
  506.4 10.2 %collective-permute-start.9 = (bf16[1,1,3,4,6272]{4,3,2,1,0:T(4,128)(2,1)S(1)}, bf16[1,1,3,4,6272]{4,3,2,1,0:T(4,128)(2,1)S(1)}, u32[]{:S(2)}, u32[]{:S(2)}) collective-permute-start(bf16[1,1,3,4,6272]{4,3,2,1,0:T(4,128)(2,1)S(1)} %get-tuple-element.110), channel_id=1, source_target_pairs={{8,0},{16,8},{24,16},{32,24},{40,32},{48,40},{56,48},{0,56},{9,1},... | collective-permute-start | bytes 451592 | tf_op jit(solution)/shard_map/ppermute | solution.py:20
  516.9 36.1 %collective-permute-start.10 = (bf16[1,1,1,4,6272]{4,3,2,1,0:T(4,128)(2,1)S(1)}, bf16[1,1,1,4,6272]{4,3,2,1,0:T(4,128)(2,1)S(1)}, u32[]{:S(2)}, u32[]{:S(2)}) collective-permute-start(bf16[1,1,1,4,6272]{4,3,2,1,0:T(4,128)(2,1)S(1)} %get-tuple-element.111), channel_id=1, source_target_pairs={{0,1},{1,2},{2,3},{3,4},{4,5},{5,6},{6,7},{7,0},{8,9},{9,10},{10,1... | collective-permute-start | bytes 150536 | tf_op jit(solution)/shard_map/ppermute | solution.py:17
  518.9 34.2 %collective-permute-start.11 = (bf16[1,1,1,4,6272]{4,3,2,1,0:T(4,128)(2,1)S(1)}, bf16[1,1,1,4,6272]{4,3,2,1,0:T(4,128)(2,1)}, u32[]{:S(2)}, u32[]{:S(2)}) collective-permute-start(bf16[1,1,1,4,6272]{4,3,2,1,0:T(4,128)(2,1)S(1)} %get-tuple-element.112), channel_id=1, source_target_pairs={{1,0},{2,1},{3,2},{4,3},{5,4},{6,5},{7,6},{0,7},{9,8},{10,9},{11,1... | collective-permute-start | bytes 150536 | tf_op jit(solution)/shard_map/ppermute | solution.py:20
  (30 other events, 115.1 us)
Sparse Core Ops, SparseCore 0:
  9.5 201.0 all-gather.5
  212.7 194.6 all-gather.3
